TPU v7x, 512 devices: a whole 4x8x8 slice. The times are simulated.
512 devices in a mesh: tm: 64 (over z_hi, y, x), head: 8 (over z_lo, core).
Axes of the slice: x: 4, y: 8, z: 8 (z_hi: 2, z_lo: 4; z = z_hi * 4 + z_lo), core: 2. Of those that a mesh axis runs over, the one named last changes fastest.
Arguments:
- frames_in: bfloat16 [64, 1024, 1024], P('tm', 'head'), may hold values from -400 to 400
- in_weight: bfloat16 [1024, 5120], P('tm', 'head'), may hold values from -0.1875 to 0.1875
- out_weight: bfloat16 [1024, 1024], replicated, may hold values from -0.1875 to 0.1875
- block_ids: int32 [1024], replicated, may hold values from 0 to 15, as said below
- block_lists: int32 [16, 4], replicated, may hold values from 0 to 15, as said below
- decays: float32 [64, 16, 16], P('tm', 'head'), may hold values from 0.3 to 1
Outputs:
- layer_out: bfloat16 [64, 1024, 1024], P('tm', 'head')
Inputs may be any that keep to these rules, and one draw needn't show every extreme that they name: `block_ids`: each of the 16 block ids is held by exactly 64 tokens. `block_lists`: row g starts with g itself, followed by 4 - 1 further blocks, all different.
All inputs are finite; a program needn't handle non-finite values.
Results may differ from a plain program's by a relative error of at most 0.0069.
Values may be sent and summed in bfloat16 or wider, within the bound.
A program may use at most 128 MiB of HBM per device.

v0:
```python
import math
import jax
import jax.numpy as jnp
from jax import lax
from jax.sharding import PartitionSpec as P

HD = 64
N = 64
TOKS = 1024
NB = 16
epsilon = 1e-06


def carried_in(shard, axis, combine, identity):
    peers, index = (lax.axis_size(axis), lax.axis_index(axis))
    everything = jax.tree.map(lambda part: lax.all_gather(part, axis), shard)
    start = jax.tree.map(
        lambda part, zero: jnp.broadcast_to(jnp.asarray(zero, part.dtype), part.shape),
        shard,
        identity,
    )

    def step(k, before):
        reached = k < index
        new = combine(before, jax.tree.map(lambda part: part[k], everything))
        return jax.tree.map(lambda a, b: jnp.where(reached, a, b), new, before)

    return lax.fori_loop(0, peers, step, start)


def head_norm(values):
    wide = values.astype(jnp.float32)
    return (wide * lax.rsqrt(jnp.mean(wide * wide, axis=-1, keepdims=True) + epsilon)).astype(
        jnp.bfloat16
    )


def combine(earlier, after_it):
    return (earlier[0] * after_it[0], after_it[0][:, :, None] * earlier[1] + after_it[1])


def body(frames_in, in_weight, out_weight, block_ids, block_lists, decays):
    frame_count, local_tokens, feature_width = frames_in.shape
    heads_here = decays.shape[1]
    groups = decays.shape[2]
    tokens = block_ids.shape[0]
    block_size = tokens // groups
    head_size = HD
    state_size = N
    selected_count = block_lists.shape[1]
    inputs_wide = frames_in.astype(jnp.float32)
    normed = (
        inputs_wide
        * lax.rsqrt(jnp.mean(inputs_wide * inputs_wide, axis=-1, keepdims=True) + epsilon)
    ).astype(jnp.bfloat16)
    full_rows = lax.all_gather(in_weight, "tm", axis=0, tiled=True)
    flat_rows = normed.reshape(frame_count * local_tokens, feature_width)
    local_flat = jnp.dot(
        flat_rows,
        lax.all_gather(full_rows, "head", axis=1, tiled=True),
        preferred_element_type=jnp.float32,
    ).astype(jnp.bfloat16)
    local_proj = local_flat.reshape(frame_count, local_tokens, local_flat.shape[1])
    projected = lax.all_to_all(local_proj, "head", split_axis=2, concat_axis=1, tiled=True)
    projected = projected.reshape(frame_count, tokens, heads_here, 5, head_size)
    sort_order = jnp.argsort(block_ids, stable=True)
    inverse_order = jnp.argsort(sort_order, stable=True)
    sorted_proj = jnp.take(projected, sort_order, axis=1).reshape(
        frame_count, groups, block_size, heads_here, 5, head_size
    )
    queries = head_norm(sorted_proj[:, :, :, :, 0])
    key_rows = head_norm(sorted_proj[:, :, :, :, 1])
    values_sorted = sorted_proj[:, :, :, :, 2]
    map_sorted = sorted_proj[:, :, :, :, 3, :state_size]
    readers_sorted = sorted_proj[:, :, :, :, 4, :state_size].astype(jnp.float32)
    chosen_keys = jnp.take(key_rows, block_lists, axis=1).reshape(
        frame_count, groups, selected_count * block_size, heads_here, head_size
    )
    chosen_values = jnp.take(values_sorted, block_lists, axis=1).reshape(
        frame_count, groups, selected_count * block_size, heads_here, head_size
    )
    updates = jnp.einsum(
        "fgshn,fgshd->fhgnd", map_sorted, values_sorted, preferred_element_type=jnp.float32
    )
    local_state = jnp.zeros((heads_here, groups, state_size, head_size), jnp.float32)
    running = jnp.ones((heads_here, groups), jnp.float32)
    frame_at = 0
    local_state = decays[frame_at][:, :, None, None] * local_state + updates[frame_at]
    running = decays[frame_at] * running
    states = [local_state]
    products = [running]
    identity = (
        jnp.ones((heads_here, groups), jnp.float32),
        jnp.zeros((heads_here, groups, state_size * head_size), jnp.float32),
    )
    carried = carried_in(
        (running, local_state.reshape(heads_here, groups, state_size * head_size)),
        "tm",
        combine,
        identity,
    )
    incoming = carried[1].reshape(heads_here, groups, state_size, head_size)
    ssm_scale = 1.0 / (N * math.sqrt(TOKS // NB))
    frame_at = 0
    full_state = states[frame_at] + products[frame_at][:, :, None, None] * incoming
    readout_sorted = (
        jnp.einsum(
            "gshn,hgnd->gshd", readers_sorted[frame_at], full_state, precision=lax.Precision.HIGHEST
        )
        * ssm_scale
    )
    scores = jnp.einsum(
        "gshd,guhd->hgsu",
        queries[frame_at],
        chosen_keys[frame_at],
        preferred_element_type=jnp.float32,
    ) / math.sqrt(head_size)
    exponent = jnp.exp(scores)
    weights = (exponent / jnp.sum(exponent, axis=-1, keepdims=True)).astype(jnp.bfloat16)
    attended = jnp.einsum(
        "hgsu,guhd->gshd", weights, chosen_values[frame_at], preferred_element_type=jnp.float32
    )
    mixed_sorted = (
        (attended + readout_sorted).astype(jnp.bfloat16).reshape(tokens, heads_here * head_size)
    )
    frames_mixed = [jnp.take(mixed_sorted, inverse_order, axis=0)]
    mixed = jnp.stack(frames_mixed, axis=0)
    token_mix = lax.all_to_all(mixed, "head", split_axis=1, concat_axis=2, tiled=True)
    result = jnp.dot(
        token_mix.reshape(frame_count * local_tokens, token_mix.shape[2]),
        out_weight,
        preferred_element_type=jnp.float32,
    )
    return result.astype(jnp.bfloat16).reshape(frame_count, local_tokens, feature_width)


def solution(mesh):
    return jax.shard_map(
        body,
        mesh=mesh,
        in_specs=(P("tm", "head", None), P("tm", "head"), P(), P(), P(), P("tm", "head", None)),
        out_specs=P("tm", "head", None),
        check_vma=False,
    )
```

profile of v0, /device:TPU:1, one launch (start us, length us, event | category | flops | bytes accessed | tf_op | source)
XLA Modules:
  0.0 990.8 jit_solution(7445949897962662394)
XLA Ops:
  7.3 138.0 %all-gather.4.cloned.1.call-done = bf16[1024,640]{1,0:T(8,128)(2,1)} async-done(((bf16[16,640]{1,0:T(8,128)(2,1)}), bf16[1024,640]{1,0:T(8,128)(2,1)}) %all-gather.4.cloned.1.call-update) | async-done | bytes 1310736 | tf_op jit(solution)/shard_map/all_gather | solution.py:56
  146.4 112.3 %all-gather.6.cloned.1.call-done = bf16[1024,5120]{1,0:T(8,128)(2,1)} async-done(((bf16[1024,640]{1,0:T(8,128)(2,1)}), bf16[1024,5120]{1,0:T(8,128)(2,1)}) %all-gather.6.cloned.1.call-update) | async-done | bytes 10485776 | tf_op jit(solution)/shard_map/all_gather | solution.py:60
  258.7 5.7 fusion.1
  264.4 4.1 copy.51
  269.1 28.9 %reduce.4 = bf16[5120,128]{1,0:T(8,128)(2,1)S(1)} reduce(bf16[5120,1,128]{2,1,0:T(2,128)(2,1)} %bitcast.84, bf16[]{:T(256)} %broadcast.155), dimensions={1}, to_apply=%bitcast.66.reduce_sub_computation | reduce | bytes 2621442
  299.2 6.9 all-to-all-start
  306.1 4.4 sort.31
  310.6 26.9 %all-to-all-done = bf16[8,2,40960]{2,1,0:T(2,128)(2,1)S(1)} async-done(((bf16[8,2,40960]{2,1,0:T(2,128)(2,1)}), bf16[8,2,40960]{2,1,0:T(2,128)(2,1)S(1)}, u32[]{:S(2)}, u32[]{:S(2)}) %all-to-all-start) | async-done | bytes 1310752 | tf_op jit(solution)/shard_map/all_to_all | solution.py:64
  337.5 3.7 reshape.273
  341.2 1.9 copy.73
  345.4 6.2 copy.53
  351.6 13.9 %gather_fusion = bf16[1024,2,5,64]{3,1,2,0:T(2,128)(2,1)} fusion(bf16[1024,2,5,64]{3,1,2,0:T(2,128)(2,1)} %copy.53, s32[1024]{0:T(1024)S(1)} %fusion.28), kind=kCustom, calls=%fused_computation.2 | custom fusion | bytes 2625536 | tf_op jit(solution)/shard_map/jit(_take)/gather | solution.py:68
  365.4 2.1 copy.54
  370.9 1.9 broadcast_add_fusion
  373.2 4.4 sort.32
  377.6 194.0 %all_gather.14 = f32[64,2,16]{2,1,0:T(2,128)S(1)} all-gather(f32[1,2,16]{2,1,0:T(2,128)S(1)} %copy-done.4), channel_id=1, replica_groups=mesh['tm'=64,'head'=8] {'tm'}, dimensions={0}, use_global_device_ids=true | all-gather | bytes 8320 | tf_op jit(solution)/shard_map/all_gather | solution.py:16
  574.4 2.1 gather_fusion.3
  576.5 2.1 slice_bitcast_fusion
  578.5 2.2 gather_fusion.2
  580.7 4.7 broadcast_select_fusion.1
  585.4 4.3 copy.59
  589.7 4.3 squeeze_reshape.7
  594.0 4.3 copy.56
  598.3 4.3 squeeze_reshape.6
  604.1 2.1 fusion.2
  606.3 1.7 fusion.13
  608.0 273.5 %all-gather.8.cloned.1.call-done = f32[64,2,16,4096]{3,2,1,0:T(8,128)} async-done(((f32[1,2,16,4096]{3,2,1,0:T(8,128)}), f32[64,2,16,4096]{3,2,1,0:T(8,128)}) %all-gather.8.cloned.1.call-update) | async-done | bytes 33554448 | tf_op jit(solution)/shard_map/all_gather | solution.py:16
  881.5 77.4 %while.14 = (s32[]{:T(128)}, f32[2,16,4096]{2,1,0:T(8,128)S(1)}, s32[]{:T(128)}, f32[64,2,16]{2,1,0:T(2,128)S(1)}, f32[64,2,16,4096]{3,2,1,0:T(8,128)}, /*index=5*/s32[]{:T(128)}, s32[]{:T(128)}) while((s32[]{:T(128)}, f32[2,16,4096]{2,1,0:T(8,128)S(1)}, s32[]{:T(128)}, f32[64,2,16]{2,1,0:T(2,128)S(1)}, ...), condition=%wide.region_7.9_spmd.clone, body=%wide.region_6.8_spmd.clone.sunk | while | flops 524292 | bytes 1573353 | solution.py:28
  960.3 3.2 fusion.5
  964.2 3.2 gather_fusion.1
  968.0 2.3 reduce.5
  970.3 12.2 %all_to_all.30 = bf16[8,2,8192]{2,1,0:T(2,128)(2,1)S(1)} all-to-all(bf16[8,2,8192]{2,1,0:T(2,128)(2,1)S(1)} %reshape.274), channel_id=1, replica_groups=mesh['tm'=64,'head'=8] {'head'}, dimensions={0} | all-to-all | bytes 524288 | tf_op jit(solution)/shard_map/all_to_all | solution.py:128
  (187 shorter events, 93.8 us)
Async XLA Ops:
  6.5 976.5 %copy-start = (bf16[1024,1024]{1,0:T(8,128)(2,1)S(1)}, bf16[1024,1024]{1,0:T(8,128)(2,1)}, u32[]{:S(2)}) copy-start(bf16[1024,1024]{1,0:T(8,128)(2,1)} %param.12) | copy-start | bytes 6291460
  6.5 138.8 %all-gather.4.cloned.1.call-start = ((), (), s32[]{:S(2)}) async-start(), calls=%async_computation.2 | async-start | bytes 1331200 | tf_op jit(solution)/shard_map/all_gather | solution.py:56
  7.3 251.5 %all-gather.6.cloned.1.call-start = ((), (), s32[]{:S(2)}) async-start(), calls=%async_computation.3 | async-start | bytes 11796480 | tf_op jit(solution)/shard_map/all_gather | solution.py:60
  298.0 8.2 copy-start.6
  298.0 12.6 %copy-start.4 = (f32[1,2,16]{2,1,0:T(2,128)S(1)}, f32[1,2,16]{2,1,0:T(2,128)}, u32[]{:S(2)}) copy-start(f32[1,2,16]{2,1,0:T(2,128)} %param.15) | copy-start | bytes 388
  299.2 38.3 %all-to-all-start = ((bf16[8,2,40960]{2,1,0:T(2,128)(2,1)}), bf16[8,2,40960]{2,1,0:T(2,128)(2,1)S(1)}, u32[]{:S(2)}, u32[]{:S(2)}) async-start(bf16[8,2,40960]{2,1,0:T(2,128)(2,1)} %reshape.272), calls=%async_computation | async-start | bytes 2621440 | tf_op jit(solution)/shard_map/all_to_all | solution.py:64
  306.1 575.3 %all-gather.8.cloned.1.call-start = ((), (), s32[]{:S(2)}) async-start(), calls=%async_computation.4 | async-start | bytes 34078720 | tf_op jit(solution)/shard_map/all_gather | solution.py:16
  367.9 1.4 copy-start.1
  369.7 3.1 copy-start.2
  369.7 3.1 copy-start.5
  602.6 3.6 copy-start.3
Sparse Core Ops, SparseCore 0:
  11.9 133.4 all-gather.3
  147.4 111.2 all-gather.5
  373.0 508.4 all-gather.7
where the time goes:
time: 995 us; the launch traced here: 991 us
  waiting for transfers between devices  551 us (55%)
  blocking collectives  206 us (21%)
  other arithmetic  127 us (13%)
  local copies, waits for them, and re-layouts  69.2 us (7%)
  matrix products  14.2 us (1%)
  between operations  13.4 us (1%)
    all_gather x1, waiting for transfers between devices, carried_in(): everything = jax.tree.map(lambda part: lax.all_gather(part, axis), shard)  273 us
    all_gather x1, blocking collectives, carried_in(): everything = jax.tree.map(lambda part: lax.all_gather(part, axis), shard)  194 us
    all_gather x1, waiting for transfers between devices, body(): full_rows = lax.all_gather(in_weight, 'tm', axis=0, tiled=True)  138 us
    all_gather x1, waiting for transfers between devices, body(): lax.all_gather(full_rows, 'head', axis=1, tiled=True)  112 us
    select_n x64, other arithmetic, step(): return jax.tree.map(lambda a, b: jnp.where(reached, a, b), new, before)  74.9 us
    unnamed x3, other arithmetic  31.2 us
    all_to_all x1, waiting for transfers between devices, body(): lax.all_to_all(local_proj, 'head', split_axis=2, concat_axis=1, tiled=True)  26.9 us
  transfers between devices with their start and end apart: 4, of which 4 were waited for; matrix products, arithmetic and copies ran while one was open for 5% of the time, Pallas kernels for 0%

commit v1 on v0

--- a/solution.py
+++ b/solution.py
@@ -53,7 +53,9 @@
         inputs_wide
         * lax.rsqrt(jnp.mean(inputs_wide * inputs_wide, axis=-1, keepdims=True) + epsilon)
     ).astype(jnp.bfloat16)
-    full_rows = lax.all_gather(in_weight, "tm", axis=0, tiled=True)
+    full_rows = jnp.concatenate(
+        lax.all_to_all(jnp.stack([in_weight] * lax.axis_size("tm")), "tm", 0, 0), axis=0
+    )
     flat_rows = normed.reshape(frame_count * local_tokens, feature_width)
     local_flat = jnp.dot(
         flat_rows,

time: 995 us -> 911 us (0.916)
  waiting for transfers between devices: 551 us -> 411 us
  blocking collectives: 206 us -> 263 us
    all_gather x1 -> x0, waiting for transfers between devices: 138 us -> none  [body(): full_rows = lax.all_gather(in_weight, 'tm', axis=0, tiled=True)]
    all_to_all x0 -> x1, blocking collectives: none -> 57.1 us  [body(): lax.all_to_all(jnp.stack([in_weight] * lax.axis_size('tm')), 'tm', 0, 0)]
  transfers between devices with their start and end apart: 4 -> 3, of which waited for: 4 -> 3; matrix products, arithmetic and copies ran while one was open for 5% -> 5% of each run, Pallas kernels for 0% -> 0%
where the time goes in v1:
time: 911 us; the launch traced here: 907 us
  waiting for transfers between devices  411 us (45%)
  blocking collectives  263 us (29%)
  other arithmetic  126 us (14%)
  local copies, waits for them, and re-layouts  70.2 us (8%)
  matrix products  14.2 us (2%)
  between operations  13.7 us (2%)
    all_gather x1, waiting for transfers between devices, carried_in(): everything = jax.tree.map(lambda part: lax.all_gather(part, axis), shard)  273 us
    all_gather x1, blocking collectives, carried_in(): everything = jax.tree.map(lambda part: lax.all_gather(part, axis), shard)  194 us
    all_gather x1, waiting for transfers between devices, body(): lax.all_gather(full_rows, 'head', axis=1, tiled=True)  110 us
    select_n x64, other arithmetic, step(): return jax.tree.map(lambda a, b: jnp.where(reached, a, b), new, before)  74.9 us
    all_to_all x1, blocking collectives, body(): lax.all_to_all(jnp.stack([in_weight] * lax.axis_size('tm')), 'tm', 0, 0)  57.1 us
    unnamed x3, other arithmetic  31.2 us
    all_to_all x1, waiting for transfers between devices, body(): lax.all_to_all(local_proj, 'head', split_axis=2, concat_axis=1, tiled=True)  26.9 us
  transfers between devices with their start and end apart: 3, of which 3 were waited for; matrix products, arithmetic and copies ran while one was open for 5% of the time, Pallas kernels for 0%

profile of v1, /device:TPU:1, one launch (start us, length us, event | category | flops | bytes accessed | tf_op | source)
XLA Modules:
  0.0 907.4 jit_solution(9664238347044555364)
XLA Ops:
  7.5 57.1 %all_to_all.35 = bf16[64,16,640]{2,1,0:T(8,128)(2,1)} all-to-all(bf16[64,16,640]{2,1,0:T(8,128)(2,1)S(1)} %stack.2), channel_id=1, replica_groups=mesh['tm'=64,'head'=8] {'tm'}, dimensions={0} | all-to-all | bytes 2621440 | tf_op jit(solution)/shard_map/all_to_all | solution.py:57
  64.8 110.1 %all-gather.3.cloned.1.call-done = bf16[1024,5120]{1,0:T(8,128)(2,1)} async-done(((bf16[1024,640]{1,0:T(8,128)(2,1)}), bf16[1024,5120]{1,0:T(8,128)(2,1)}) %all-gather.3.cloned.1.call-update) | async-done | bytes 10485776 | tf_op jit(solution)/shard_map/all_gather | solution.py:62
  175.0 5.7 fusion.1
  180.6 4.1 copy.51
  185.3 28.9 %reduce.4 = bf16[5120,128]{1,0:T(8,128)(2,1)S(1)} reduce(bf16[5120,1,128]{2,1,0:T(2,128)(2,1)} %bitcast.85, bf16[]{:T(256)} %broadcast.157), dimensions={1}, to_apply=%bitcast.67.reduce_sub_computation | reduce | bytes 2621442
  215.5 6.9 all-to-all-start.1
  222.4 4.4 sort.31
  226.9 26.9 %all-to-all-done.1 = bf16[8,2,40960]{2,1,0:T(2,128)(2,1)S(1)} async-done(((bf16[8,2,40960]{2,1,0:T(2,128)(2,1)}), bf16[8,2,40960]{2,1,0:T(2,128)(2,1)S(1)}, u32[]{:S(2)}, u32[]{:S(2)}) %all-to-all-start.1) | async-done | bytes 1310752 | tf_op jit(solution)/shard_map/all_to_all | solution.py:66
  253.8 3.7 reshape.279
  257.4 1.9 copy.73
  261.6 6.2 copy.53
  267.8 13.9 %gather_fusion = bf16[1024,2,5,64]{3,1,2,0:T(2,128)(2,1)} fusion(bf16[1024,2,5,64]{3,1,2,0:T(2,128)(2,1)} %copy.53, s32[1024]{0:T(1024)S(1)} %fusion.28), kind=kCustom, calls=%fused_computation.2 | custom fusion | bytes 2625536 | tf_op jit(solution)/shard_map/jit(_take)/gather | solution.py:70
  281.7 2.1 copy.54
  287.2 1.9 broadcast_add_fusion
  289.4 4.4 sort.32
  293.8 194.0 %all_gather.10 = f32[64,2,16]{2,1,0:T(2,128)S(1)} all-gather(f32[1,2,16]{2,1,0:T(2,128)S(1)} %copy-done.5), channel_id=1, replica_groups=mesh['tm'=64,'head'=8] {'tm'}, dimensions={0}, use_global_device_ids=true | all-gather | bytes 8320 | tf_op jit(solution)/shard_map/all_gather | solution.py:16
  490.6 2.1 gather_fusion.3
  492.7 2.1 slice_bitcast_fusion
  494.8 2.2 gather_fusion.2
  497.0 4.7 broadcast_select_fusion.1
  501.7 4.3 copy.59
  506.0 4.3 squeeze_reshape.7
  510.3 4.3 copy.56
  514.6 4.3 squeeze_reshape.6
  520.4 2.1 fusion.2
  522.5 1.7 fusion.13
  524.2 273.5 %all-gather.5.cloned.1.call-done = f32[64,2,16,4096]{3,2,1,0:T(8,128)} async-done(((f32[1,2,16,4096]{3,2,1,0:T(8,128)}), f32[64,2,16,4096]{3,2,1,0:T(8,128)}) %all-gather.5.cloned.1.call-update) | async-done | bytes 33554448 | tf_op jit(solution)/shard_map/all_gather | solution.py:16
  797.7 77.4 %while.14 = (s32[]{:T(128)}, f32[2,16,4096]{2,1,0:T(8,128)S(1)}, s32[]{:T(128)}, f32[64,2,16]{2,1,0:T(2,128)S(1)}, f32[64,2,16,4096]{3,2,1,0:T(8,128)}, /*index=5*/s32[]{:T(128)}, s32[]{:T(128)}) while((s32[]{:T(128)}, f32[2,16,4096]{2,1,0:T(8,128)S(1)}, s32[]{:T(128)}, f32[64,2,16]{2,1,0:T(2,128)S(1)}, ...), condition=%wide.region_7.9_spmd.clone, body=%wide.region_6.8_spmd.clone.sunk | while | flops 524292 | bytes 1573353 | solution.py:28
  876.6 3.2 fusion.5
  880.4 3.2 gather_fusion.1
  884.3 2.3 reduce.5
  886.6 12.2 %all_to_all.36 = bf16[8,2,8192]{2,1,0:T(2,128)(2,1)S(1)} all-to-all(bf16[8,2,8192]{2,1,0:T(2,128)(2,1)S(1)} %reshape.280), channel_id=1, replica_groups=mesh['tm'=64,'head'=8] {'head'}, dimensions={0} | all-to-all | bytes 524288 | tf_op jit(solution)/shard_map/all_to_all | solution.py:130
  (188 shorter events, 93.0 us)
Async XLA Ops:
  6.5 892.8 %copy-start = (bf16[1024,1024]{1,0:T(8,128)(2,1)S(1)}, bf16[1024,1024]{1,0:T(8,128)(2,1)}, u32[]{:S(2)}) copy-start(bf16[1024,1024]{1,0:T(8,128)(2,1)} %param.12) | copy-start | bytes 6291460
  6.5 168.4 %all-gather.3.cloned.1.call-start = ((), (), s32[]{:S(2)}) async-start(), calls=%async_computation.3 | async-start | bytes 11796480 | tf_op jit(solution)/shard_map/all_gather | solution.py:62
  7.5 57.2 %copy-start.3 = (bf16[1,128,1024]{2,1,0:T(8,128)(2,1)S(1)}, bf16[1,128,1024]{2,1,0:T(8,128)(2,1)}, u32[]{:S(2)}) copy-start(bf16[1,128,1024]{2,1,0:T(8,128)(2,1)} %param.10) | copy-start | bytes 786436
  214.2 8.2 copy-start.7
  214.2 12.6 %copy-start.5 = (f32[1,2,16]{2,1,0:T(2,128)S(1)}, f32[1,2,16]{2,1,0:T(2,128)}, u32[]{:S(2)}) copy-start(f32[1,2,16]{2,1,0:T(2,128)} %param.15) | copy-start | bytes 388
  215.5 38.3 %all-to-all-start.1 = ((bf16[8,2,40960]{2,1,0:T(2,128)(2,1)}), bf16[8,2,40960]{2,1,0:T(2,128)(2,1)S(1)}, u32[]{:S(2)}, u32[]{:S(2)}) async-start(bf16[8,2,40960]{2,1,0:T(2,128)(2,1)} %reshape.278), calls=%async_computation.1 | async-start | bytes 2621440 | tf_op jit(solution)/shard_map/all_to_all | solution.py:66
  222.4 575.3 %all-gather.5.cloned.1.call-start = ((), (), s32[]{:S(2)}) async-start(), calls=%async_computation.4 | async-start | bytes 34078720 | tf_op jit(solution)/shard_map/all_gather | solution.py:16
  284.2 1.4 copy-start.1
  286.0 3.1 copy-start.2
  286.0 3.1 copy-start.6
  518.9 3.6 copy-start.4
Sparse Core Ops, SparseCore 0:
  64.8 110.1 all-gather.2
  289.2 508.4 all-gather.4
